TPU v7x, 32 devices: a whole 2x2x4 slice. The times are simulated.
32 devices in a mesh: dp: 2 (over core), seq: 16 (over z, y, x).
Axes of the slice: x: 2, y: 2, z: 4, core: 2. Of those that a mesh axis runs over, the one named last changes fastest.
Arguments:
- queries: bfloat16 [2, 2048, 512], P('dp', 'seq'), may hold values from -6 to 6
- keys: bfloat16 [2, 2048, 512], P('dp', 'seq'), may hold values from -6 to 6
- values: bfloat16 [2, 2048, 512], P('dp', 'seq'), may hold values from -12 to 12
- residual: bfloat16 [2, 2048, 1024], P('dp', 'seq'), may hold values from -3 to 3
- out_proj: bfloat16 [512, 1024], replicated, may hold values from -0.25 to 0.25
- conv_in: bfloat16 [1024, 2048], P(None, 'seq'), may hold values from -0.1875 to 0.1875
- conv_out: bfloat16 [1024, 1024], replicated, may hold values from -0.1875 to 0.1875
- depth_kernel: bfloat16 [31, 1024], replicated, may hold values from -1 to 1
- norm_gain: float32 [1024], replicated, may hold values from 0.25 to 1.75
- cotangent: bfloat16 [2, 2048, 1024], P('dp', 'seq'), may hold values from -6 to 6
Outputs:
- layer_out: bfloat16 [2, 2048, 1024], P('dp', 'seq')
- grad_mid: bfloat16 [2, 2048, 1024], P('dp', 'seq')
- grad_out_proj: float32 [512, 1024], P('seq')
- grad_kernel: float32 [31, 1024], replicated
All inputs are finite; a program needn't handle non-finite values.
Results may differ from a plain program's by a relative error of at most 0.015.
Values may be sent and summed in bfloat16 or wider, within the bound.
A program may use at most 128 MiB of HBM per device.

v0:
```python
import math

import jax
import jax.numpy as jnp
from jax import lax
from jax.sharding import PartitionSpec as P

HEADS = 8
DH = 64
KW = 31


norm_epsilon = 1e-05


def padded_2(cells, sides, width):
    for axis, dim in sides:
        count = lax.axis_size(axis)
        ends = count - 1
        head = lax.slice_in_dim(cells, 0, width, axis=dim)
        tail = lax.slice_in_dim(cells, cells.shape[dim] - width, cells.shape[dim], axis=dim)
        cells = jnp.concatenate(
            [
                lax.ppermute(tail, axis, [(i, (i + 1) % count) for i in range(ends)]),
                cells,
                lax.ppermute(head, axis, [((i + 1) % count, i) for i in range(ends)]),
            ],
            axis=dim,
        )
    return cells


def attend_one(triple):
    query, key_rows, value_rows = triple
    length = query.shape[0]
    block = math.gcd(length, 512)
    query_blocks = query.reshape(length // block, block, query.shape[1])

    def one_block(query_block):
        scores = lax.dot_general(
            query_block, key_rows, (((1,), (1,)), ((), ())), preferred_element_type=jnp.float32
        ) * DH ** (-0.5)
        highest = jnp.max(scores, axis=1, keepdims=True)
        expo = jnp.exp(scores - highest)
        total = jnp.sum(expo, axis=1, keepdims=True)
        weights = expo.astype(jnp.bfloat16)
        mixed = jnp.dot(weights, value_rows, preferred_element_type=jnp.float32)
        return (mixed / total).astype(jnp.bfloat16)

    return lax.map(one_block, query_blocks).reshape(length, query.shape[1])


def attend_items(pieces):
    query_all, key_all, value_all = pieces
    return lax.map(attend_one, (query_all[0], key_all[0], value_all[0]))[None]


def layer_norm(mid):
    wide = mid.astype(jnp.float32)
    centered = wide - jnp.mean(wide, axis=-1, keepdims=True)
    rscale = lax.rsqrt(jnp.mean(centered * centered, axis=-1, keepdims=True) + norm_epsilon)
    return (centered * rscale, rscale)


def depth_forward(padded, kernel, rows):
    total = jnp.zeros((padded.shape[0], rows, padded.shape[2]), jnp.float32)
    for offset in range(KW):
        total = total + kernel[offset].astype(jnp.float32) * padded[
            :, offset : offset + rows
        ].astype(jnp.float32)
    return total


def depth_backward(padded, kernel, rows):
    total = jnp.zeros((padded.shape[0], rows, padded.shape[2]), jnp.float32)
    reach = (KW - 1) // 2
    for offset in range(KW):
        begin = 2 * reach - offset
        total = total + kernel[offset].astype(jnp.float32) * padded[:, begin : begin + rows].astype(
            jnp.float32
        )
    return total


def kernel_terms(padded, grad_conv, rows):
    terms = []
    for offset in range(KW):
        product = padded[:, offset : offset + rows].astype(jnp.float32) * grad_conv.astype(
            jnp.float32
        )
        terms.append(jnp.sum(product, axis=(0, 1)))
    return jnp.stack(terms, axis=0)


def body(
    queries, keys, values, residual, out_proj, conv_in, conv_out, depth_kernel, norm_gain, cotangent
):
    seq_count = lax.axis_size("seq")
    group = seq_count // HEADS
    batch, rows, width = queries.shape
    model = residual.shape[2]
    part = rows // group
    flat = batch * rows
    reach = (KW - 1) // 2
    query_send = (
        queries.reshape(batch, group, part, HEADS, DH)
        .transpose(3, 1, 0, 2, 4)
        .reshape(seq_count, batch, part, DH)
    )
    key_heads = keys.reshape(batch, rows, HEADS, DH).transpose(2, 0, 1, 3)
    value_heads = values.reshape(batch, rows, HEADS, DH).transpose(2, 0, 1, 3)
    key_send = jnp.broadcast_to(key_heads[:, None], (HEADS, group, batch, rows, DH)).reshape(
        seq_count, batch, rows, DH
    )
    value_send = jnp.broadcast_to(value_heads[:, None], (HEADS, group, batch, rows, DH)).reshape(
        seq_count, batch, rows, DH
    )
    attended_heads = attend_items(
        (
            lax.all_to_all(query_send, "seq", split_axis=0, concat_axis=2, tiled=True),
            lax.all_to_all(key_send, "seq", split_axis=0, concat_axis=2, tiled=True),
            lax.all_to_all(value_send, "seq", split_axis=0, concat_axis=2, tiled=True),
        )
    )
    returned = lax.all_to_all(
        attended_heads.reshape(1, batch, seq_count, part, DH),
        "seq",
        split_axis=2,
        concat_axis=0,
        tiled=True,
    )
    attended = (
        returned.reshape(HEADS, group, batch, part, DH)
        .transpose(2, 1, 3, 0, 4)
        .reshape(flat, width)
    )
    flat_resid = residual.reshape(flat, model).astype(jnp.float32)
    mid = (flat_resid + jnp.dot(attended, out_proj, preferred_element_type=jnp.float32)).astype(
        jnp.bfloat16
    )
    hat, rscale = layer_norm(mid)
    normed = (hat * norm_gain).astype(jnp.bfloat16)
    proj = jnp.dot(
        normed,
        lax.all_gather(conv_in, "seq", axis=1, tiled=True),
        preferred_element_type=jnp.float32,
    )
    value_half = proj[:, :model]
    gate_half = jax.nn.sigmoid(proj[:, model:])
    gated = (value_half * gate_half).astype(jnp.bfloat16).reshape(batch, rows, model)
    padded = padded_2(gated, (("seq", 1),), reach)
    conv = depth_forward(padded, depth_kernel, rows)
    act = (conv * jax.nn.sigmoid(conv)).astype(jnp.bfloat16).reshape(flat, model)
    layer_out = (
        mid.astype(jnp.float32) + jnp.dot(act, conv_out, preferred_element_type=jnp.float32)
    ).astype(jnp.bfloat16)
    flat_cot = cotangent.reshape(flat, model)
    grad_act = lax.dot_general(
        flat_cot, conv_out, (((1,), (1,)), ((), ())), preferred_element_type=jnp.float32
    )
    sig_conv = jax.nn.sigmoid(conv).reshape(flat, model)
    conv_flat = conv.reshape(flat, model)
    grad_conv = (
        (grad_act * sig_conv * (1.0 + conv_flat * (1.0 - sig_conv)))
        .astype(jnp.bfloat16)
        .reshape(batch, rows, model)
    )
    grad_padded = padded_2(grad_conv, (("seq", 1),), reach)
    grad_gated = depth_backward(grad_padded, depth_kernel, rows).reshape(flat, model)
    grad_kernel = lax.psum(kernel_terms(padded, grad_conv, rows), ("dp", "seq"))
    grad_proj = jnp.concatenate(
        [grad_gated * gate_half, grad_gated * value_half * gate_half * (1.0 - gate_half)], axis=1
    ).astype(jnp.bfloat16)
    grad_normed = lax.dot_general(
        grad_proj,
        lax.all_gather(conv_in, "seq", axis=1, tiled=True),
        (((1,), (1,)), ((), ())),
        preferred_element_type=jnp.float32,
    )
    scaled = grad_normed * norm_gain
    inner = (
        scaled
        - jnp.mean(scaled, axis=1, keepdims=True)
        - hat * jnp.mean(scaled * hat, axis=1, keepdims=True)
    )
    grad_mid = (flat_cot.astype(jnp.float32) + rscale * inner).astype(jnp.bfloat16)
    partial_rows = lax.psum_scatter(
        lax.dot_general(
            attended, grad_mid, (((0,), (0,)), ((), ())), preferred_element_type=jnp.float32
        ),
        "seq",
        scatter_dimension=0,
        tiled=True,
    )
    grad_out_proj = lax.psum(partial_rows.astype(jnp.bfloat16), "dp").astype(jnp.float32)
    return (
        layer_out.reshape(batch, rows, model),
        grad_mid.reshape(batch, rows, model),
        grad_out_proj,
        grad_kernel,
    )


def solution(mesh):
    return jax.shard_map(
        body,
        mesh=mesh,
        in_specs=(
            P("dp", "seq", None),
            P("dp", "seq", None),
            P("dp", "seq", None),
            P("dp", "seq", None),
            P(),
            P(None, "seq"),
            P(),
            P(),
            P(),
            P("dp", "seq", None),
        ),
        out_specs=(P("dp", "seq", None), P("dp", "seq", None), P("seq", None), P()),
        check_vma=False,
    )
```

profile of v0, /device:TPU:13, one launch (start us, length us, event | category | flops | bytes accessed | tf_op | source)
XLA Modules:
  0.0 379.1 jit_solution(8444555819019759664)
XLA Ops:
  7.9 1.1 reshape.406
  9.1 0.9 reshape.454
  10.0 6.6 %all-to-all-start = ((bf16[16,2,2048]{2,1,0:T(2,128)(2,1)}), bf16[16,2,2048]{2,1,0:T(2,128)(2,1)S(1)}, u32[]{:S(2)}, u32[]{:S(2)}) async-start(bf16[16,2,2048]{2,1,0:T(2,128)(2,1)} %reshape.454), calls=%async_computation | async-start | bytes 262144 | tf_op jit(solution)/shard_map/all_to_all | solution.py:120
  16.6 1.0 copy.31
  17.6 4.2 %all-to-all-done = bf16[16,2,2048]{2,1,0:T(2,128)(2,1)S(1)} async-done(((bf16[16,2,2048]{2,1,0:T(2,128)(2,1)}), bf16[16,2,2048]{2,1,0:T(2,128)(2,1)S(1)}, u32[]{:S(2)}, u32[]{:S(2)}) %all-to-all-start) | async-done | bytes 131104 | tf_op jit(solution)/shard_map/all_to_all | solution.py:120
  22.6 4.9 %all-to-all-start.1 = ((bf16[16,1,128,64]{2,3,1,0:T(8,128)(2,1)}), bf16[16,1,128,64]{2,3,1,0:T(8,128)(2,1)S(1)}, u32[]{:S(2)}, u32[]{:S(2)}) async-start(bf16[16,1,128,64]{2,3,1,0:T(8,128)(2,1)} %bitcast.9), calls=%async_computation.1 | async-start | bytes 524288 | tf_op jit(solution)/shard_map/all_to_all | solution.py:121
  27.4 1.0 copy.33
  28.5 5.2 %all-to-all-done.1 = bf16[16,1,128,64]{2,3,1,0:T(8,128)(2,1)S(1)} async-done(((bf16[16,1,128,64]{2,3,1,0:T(8,128)(2,1)}), bf16[16,1,128,64]{2,3,1,0:T(8,128)(2,1)S(1)}, u32[]{:S(2)}, u32[]{:S(2)}) %all-to-all-start.1) | async-done | bytes 262176 | tf_op jit(solution)/shard_map/all_to_all | solution.py:121
  34.4 6.2 %all-to-all-start.2 = ((bf16[16,1,128,64]{2,3,1,0:T(8,128)(2,1)}), bf16[16,1,128,64]{2,3,1,0:T(8,128)(2,1)}, u32[]{:S(2)}, u32[]{:S(2)}) async-start(bf16[16,1,128,64]{2,3,1,0:T(8,128)(2,1)} %bitcast.14), calls=%async_computation.2 | async-start | bytes 524288 | tf_op jit(solution)/shard_map/all_to_all | solution.py:122
  41.1 9.2 %all-to-all-done.2 = bf16[16,1,128,64]{2,3,1,0:T(8,128)(2,1)} async-done(((bf16[16,1,128,64]{2,3,1,0:T(8,128)(2,1)}), bf16[16,1,128,64]{2,3,1,0:T(8,128)(2,1)}, u32[]{:S(2)}, u32[]{:S(2)}) %all-to-all-start.2) | async-done | bytes 262176 | tf_op jit(solution)/shard_map/all_to_all | solution.py:122
  50.3 1.2 copy.41
  51.5 6.5 %while.17 = (s32[]{:T(128)}, bf16[2,512,64]{1,2,0:T(8,128)(2,1)}, bf16[2,512,64]{2,1,0:T(8,128)(2,1)S(1)}, bf16[2048,64]{1,0:T(8,128)(2,1)S(1)}, bf16[2048,64]{1,0:T(8,128)(2,1)S(1)}, /*index=5*/s32[]{:T(128)}) while((s32[]{:T(128)}, bf16[2,512,64]{1,2,0:T(8,128)(2,1)}, bf16[2,512,64]{2,1,0:T(8,128)(2,1)S(1)}, bf16[2048,64]{1,0:T(8,128)(2,1)S(1)}, ...), condition=%wide.region_3.4_spmd, body=%wide.region_0.3_spmd.sunk | while | flops 276888576 | bytes 13576777 | solution.py:50
  51.5 0.8 multiply_reduce_fusion.4
  52.3 0.8 fusion.236
  53.1 1.6 fusion.237
  54.8 0.8 multiply_reduce_fusion.4
  55.5 0.8 fusion.236
  56.4 1.6 fusion.237
  58.0 1.1 copy.37
  59.3 0.9 reshape.456
  60.2 10.4 %all-to-all-start.3 = ((bf16[16,2,2048]{2,1,0:T(2,128)(2,1)}), bf16[16,2,2048]{2,1,0:T(2,128)(2,1)S(1)}, u32[]{:S(2)}, u32[]{:S(2)}) async-start(bf16[16,2,2048]{2,1,0:T(2,128)(2,1)} %reshape.456), calls=%async_computation.3 | async-start | bytes 262144 | tf_op jit(solution)/shard_map/all_to_all | solution.py:125
  70.9 10.3 %all-to-all-done.3 = bf16[16,2,2048]{2,1,0:T(2,128)(2,1)S(1)} async-done(((bf16[16,2,2048]{2,1,0:T(2,128)(2,1)}), bf16[16,2,2048]{2,1,0:T(2,128)(2,1)S(1)}, u32[]{:S(2)}, u32[]{:S(2)}) %all-to-all-start.3) | async-done | bytes 131104 | tf_op jit(solution)/shard_map/all_to_all | solution.py:125
  81.9 1.7 fusion.215
  83.6 0.8 copy-done.2
  84.5 21.6 %all-gather.2.cloned.1.call-done = bf16[1024,2048]{1,0:T(8,128)(2,1)} async-done(((bf16[1024,128]{1,0:T(8,128)(2,1)}), bf16[1024,2048]{1,0:T(8,128)(2,1)}) %all-gather.2.cloned.1.call-update) | async-done | bytes 4194320 | tf_op jit(solution)/shard_map/all_gather | solution.py:145
  106.2 3.2 fusion.147
  109.5 2.2 collective-permute-start
  111.7 4.0 %collective-permute-start.1 = (bf16[1,15,1024]{2,1,0:T(8,128)(2,1)S(1)}, bf16[1,15,1024]{2,1,0:T(8,128)(2,1)S(1)}, u32[]{:S(2)}, u32[]{:S(2)}) collective-permute-start(bf16[1,15,1024]{2,1,0:T(8,128)(2,1)S(1)} %get-tuple-element.100), channel_id=1, source_target_pairs={{1,0},{2,1},{3,2},{4,3},{5,4},{6,5},{7,6},{8,7},{9,8},{10,9},{11,1... | collective-permute-start | bytes 92168 | tf_op jit(solution)/shard_map/ppermute | solution.py:26
  115.8 3.0 collective-permute-done.1
  119.0 2.6 fusion.87
  121.8 1.9 fusion.101
  123.8 2.6 collective-permute-start.2
  126.4 4.6 %collective-permute-start.3 = (bf16[1,15,1024]{2,1,0:T(8,128)(2,1)S(1)}, bf16[1,15,1024]{2,1,0:T(8,128)(2,1)S(1)}, u32[]{:S(2)}, u32[]{:S(2)}) collective-permute-start(bf16[1,15,1024]{2,1,0:T(8,128)(2,1)S(1)} %get-tuple-element.99), channel_id=1, source_target_pairs={{0,1},{1,2},{2,3},{3,4},{4,5},{5,6},{6,7},{7,8},{8,9},{9,10},{10,1... | collective-permute-start | bytes 92168 | tf_op jit(solution)/shard_map/ppermute | solution.py:24
  131.0 1.2 collective-permute-done.3
  132.4 2.6 fusion.142
  135.3 1.6 fusion.211
  137.9 1.8 fusion.216
  139.8 2.5 fusion.116
  142.3 3.5 fusion.117
  145.8 3.7 fusion.102
  149.5 57.0 %reduce-scatter.2.cloned.1.call-done = f32[32,1024]{1,0:T(8,128)} async-done(((f32[512,1024]{1,0:T(8,128)}), f32[32,1024]{1,0:T(8,128)}) %reduce-scatter.2.cloned.1.call-update) | async-done | bytes 131088 | tf_op jit(solution)/shard_map/reduce_scatter | solution.py:187
  206.5 1.5 convert_element_type.775
  208.3 2.7 stack.127
  211.0 2.4 fusion.26
  213.4 30.7 %all-reduce.3.cloned.1.call-done = bf16[32,1024]{1,0:T(8,128)(2,1)} async-done(((bf16[32,1024]{1,0:T(8,128)(2,1)}), bf16[32,1024]{1,0:T(8,128)(2,1)}) %all-reduce.3.cloned.1.call-update) | async-done | bytes 65552 | tf_op jit(solution)/shard_map/psum | solution.py:195
  244.0 1.5 convert_element_type.776
  245.6 125.4 %all-reduce.5.cloned.1.call-done = f32[31,1024]{1,0:T(8,128)} async-done(((f32[31,1024]{1,0:T(8,128)}), f32[31,1024]{1,0:T(8,128)}) %all-reduce.5.cloned.1.call-update) | async-done | bytes 126992 | tf_op jit(solution)/shard_map/psum | solution.py:170
  371.0 1.6 copy.57
  (138 shorter events, 5.9 us)
Async XLA Ops:
  7.2 114.4 %copy-start = (bf16[1024,1024]{1,0:T(8,128)(2,1)S(1)}, bf16[1024,1024]{1,0:T(8,128)(2,1)}, u32[]{:S(2)}) copy-start(bf16[1024,1024]{1,0:T(8,128)(2,1)} %param.18) | copy-start | bytes 6291460
  7.2 99.0 %all-gather.2.cloned.1.call-start = ((), (), s32[]{:S(2)}) async-start(), calls=%async_computation.5 | async-start | bytes 4456448 | tf_op jit(solution)/shard_map/all_gather | solution.py:145
  10.0 11.8 %all-to-all-start = ((bf16[16,2,2048]{2,1,0:T(2,128)(2,1)}), bf16[16,2,2048]{2,1,0:T(2,128)(2,1)S(1)}, u32[]{:S(2)}, u32[]{:S(2)}) async-start(bf16[16,2,2048]{2,1,0:T(2,128)(2,1)} %reshape.454), calls=%async_computation | async-start | bytes 262144 | tf_op jit(solution)/shard_map/all_to_all | solution.py:120
  22.6 11.1 %all-to-all-start.1 = ((bf16[16,1,128,64]{2,3,1,0:T(8,128)(2,1)}), bf16[16,1,128,64]{2,3,1,0:T(8,128)(2,1)S(1)}, u32[]{:S(2)}, u32[]{:S(2)}) async-start(bf16[16,1,128,64]{2,3,1,0:T(8,128)(2,1)} %bitcast.9), calls=%async_computation.1 | async-start | bytes 524288 | tf_op jit(solution)/shard_map/all_to_all | solution.py:121
  34.4 15.9 %all-to-all-start.2 = ((bf16[16,1,128,64]{2,3,1,0:T(8,128)(2,1)}), bf16[16,1,128,64]{2,3,1,0:T(8,128)(2,1)}, u32[]{:S(2)}, u32[]{:S(2)}) async-start(bf16[16,1,128,64]{2,3,1,0:T(8,128)(2,1)} %bitcast.14), calls=%async_computation.2 | async-start | bytes 524288 | tf_op jit(solution)/shard_map/all_to_all | solution.py:122
  51.5 19.2 %copy-start.9 = (bf16[31,1024]{1,0:T(8,128)(2,1)S(1)}, bf16[31,1024]{1,0:T(8,128)(2,1)}, u32[]{:S(2)}) copy-start(bf16[31,1024]{1,0:T(8,128)(2,1)} %param.19) | copy-start | bytes 190468
  58.0 48.2 %copy-start.41 = (f32[1024]{0:T(1024)S(1)}, f32[1024]{0:T(1024)}, u32[]{:S(2)}) copy-start(f32[1024]{0:T(1024)} %param.20) | copy-start | bytes 12292
  60.2 21.0 %all-to-all-start.3 = ((bf16[16,2,2048]{2,1,0:T(2,128)(2,1)}), bf16[16,2,2048]{2,1,0:T(2,128)(2,1)S(1)}, u32[]{:S(2)}, u32[]{:S(2)}) async-start(bf16[16,2,2048]{2,1,0:T(2,128)(2,1)} %reshape.456), calls=%async_computation.3 | async-start | bytes 262144 | tf_op jit(solution)/shard_map/all_to_all | solution.py:125
  70.7 135.8 %reduce-scatter.2.cloned.1.call-start = ((), (), s32[]{:S(2)}) async-start(), calls=%async_computation.6 | async-start | bytes 2228224 | tf_op jit(solution)/shard_map/reduce_scatter | solution.py:187
  70.8 48.0 %copy-start.11 = (f32[1,1024]{1,0:T(1,128)}, f32[1,1024]{1,0:T(1,128)S(1)}, u32[]{:S(2)}) copy-start(f32[1,1024]{1,0:T(1,128)S(1)} %get-tuple-element.106) | copy-start | bytes 12292
  70.8 48.0 %copy-start.13 = (f32[1,1024]{1,0:T(1,128)}, f32[1,1024]{1,0:T(1,128)S(1)}, u32[]{:S(2)}) copy-start(f32[1,1024]{1,0:T(1,128)S(1)} %get-tuple-element.107) | copy-start | bytes 12292
  70.8 48.0 %copy-start.15 = (f32[1,1024]{1,0:T(1,128)}, f32[1,1024]{1,0:T(1,128)S(1)}, u32[]{:S(2)}) copy-start(f32[1,1024]{1,0:T(1,128)S(1)} %get-tuple-element.108) | copy-start | bytes 12292
  70.8 48.0 %copy-start.17 = (f32[1,1024]{1,0:T(1,128)}, f32[1,1024]{1,0:T(1,128)S(1)}, u32[]{:S(2)}) copy-start(f32[1,1024]{1,0:T(1,128)S(1)} %get-tuple-element.109) | copy-start | bytes 12292
  70.8 48.0 %copy-start.19 = (f32[1,1024]{1,0:T(1,128)}, f32[1,1024]{1,0:T(1,128)S(1)}, u32[]{:S(2)}) copy-start(f32[1,1024]{1,0:T(1,128)S(1)} %get-tuple-element.110) | copy-start | bytes 12292
  70.8 48.0 %copy-start.21 = (f32[1,1024]{1,0:T(1,128)}, f32[1,1024]{1,0:T(1,128)S(1)}, u32[]{:S(2)}) copy-start(f32[1,1024]{1,0:T(1,128)S(1)} %get-tuple-element.111) | copy-start | bytes 12292
  70.8 48.0 %copy-start.23 = (f32[1,1024]{1,0:T(1,128)}, f32[1,1024]{1,0:T(1,128)S(1)}, u32[]{:S(2)}) copy-start(f32[1,1024]{1,0:T(1,128)S(1)} %get-tuple-element.112) | copy-start | bytes 12292
  70.8 48.0 %copy-start.25 = (f32[1,1024]{1,0:T(1,128)}, f32[1,1024]{1,0:T(1,128)S(1)}, u32[]{:S(2)}) copy-start(f32[1,1024]{1,0:T(1,128)S(1)} %get-tuple-element.113) | copy-start | bytes 12292
  70.9 48.0 %copy-start.27 = (f32[1,1024]{1,0:T(1,128)}, f32[1,1024]{1,0:T(1,128)S(1)}, u32[]{:S(2)}) copy-start(f32[1,1024]{1,0:T(1,128)S(1)} %get-tuple-element.114) | copy-start | bytes 12292
  70.9 48.0 %copy-start.29 = (f32[1,1024]{1,0:T(1,128)}, f32[1,1024]{1,0:T(1,128)S(1)}, u32[]{:S(2)}) copy-start(f32[1,1024]{1,0:T(1,128)S(1)} %get-tuple-element.115) | copy-start | bytes 12292
  70.9 48.0 %copy-start.31 = (f32[1,1024]{1,0:T(1,128)}, f32[1,1024]{1,0:T(1,128)S(1)}, u32[]{:S(2)}) copy-start(f32[1,1024]{1,0:T(1,128)S(1)} %get-tuple-element.116) | copy-start | bytes 12292
  70.9 48.0 %copy-start.33 = (f32[1,1024]{1,0:T(1,128)}, f32[1,1024]{1,0:T(1,128)S(1)}, u32[]{:S(2)}) copy-start(f32[1,1024]{1,0:T(1,128)S(1)} %get-tuple-element.117) | copy-start | bytes 12292
  70.9 48.0 %copy-start.35 = (f32[1,1024]{1,0:T(1,128)}, f32[1,1024]{1,0:T(1,128)S(1)}, u32[]{:S(2)}) copy-start(f32[1,1024]{1,0:T(1,128)S(1)} %get-tuple-element.118) | copy-start | bytes 12292
  70.9 48.0 %copy-start.37 = (f32[1,1024]{1,0:T(1,128)}, f32[1,1024]{1,0:T(1,128)S(1)}, u32[]{:S(2)}) copy-start(f32[1,1024]{1,0:T(1,128)S(1)} %get-tuple-element.119) | copy-start | bytes 12292
  70.9 48.0 %copy-start.39 = (f32[1,1024]{1,0:T(1,128)}, f32[1,1024]{1,0:T(1,128)S(1)}, u32[]{:S(2)}) copy-start(f32[1,1024]{1,0:T(1,128)S(1)} %get-tuple-element.120) | copy-start | bytes 12292
  83.6 25.8 %copy-start.43 = (f32[128]{0:T(128)}, f32[128]{0:T(128)S(1)}, u32[]{:S(2)}) copy-start(f32[128]{0:T(128)S(1)} %broadcast_multiply_fusion.2) | copy-start | bytes 1540
  84.5 24.8 %copy-start.45 = (f32[128]{0:T(128)}, f32[128]{0:T(128)S(1)}, u32[]{:S(2)}) copy-start(f32[128]{0:T(128)S(1)} %add_rsqrt_fusion) | copy-start | bytes 1540
  106.2 15.4 %copy-start.8 = (bf16[1,128,1024]{2,1,0:T(8,128)(2,1)S(1)}, bf16[1,128,1024]{2,1,0:T(8,128)(2,1)}, u32[]{:S(2)}) copy-start(bf16[1,128,1024]{2,1,0:T(8,128)(2,1)} %param.21) | copy-start | bytes 786436
  109.5 12.1 %copy-start.4 = (bf16[1,128,1024]{2,1,0:T(8,128)(2,1)}, bf16[1,128,1024]{2,1,0:T(8,128)(2,1)S(1)}, u32[]{:S(2)}) copy-start(bf16[1,128,1024]{2,1,0:T(8,128)(2,1)S(1)} %fusion.227) | copy-start | bytes 786436
  109.5 6.2 %collective-permute-start = (bf16[1,15,1024]{2,1,0:T(8,128)(2,1)S(1)}, bf16[1,15,1024]{2,1,0:T(8,128)(2,1)S(1)}, u32[]{:S(2)}, u32[]{:S(2)}) collective-permute-start(bf16[1,15,1024]{2,1,0:T(8,128)(2,1)S(1)} %get-tuple-element.101), channel_id=1, source_target_pairs={{0,1},{1,2},{2,3},{3,4},{4,5},{5,6},{6,7},{7,8},{8,9},{9,10},{10,1... | collective-permute-start | bytes 92168 | tf_op jit(solution)/shard_map/ppermute | solution.py:24
  111.7 7.1 %collective-permute-start.1 = (bf16[1,15,1024]{2,1,0:T(8,128)(2,1)S(1)}, bf16[1,15,1024]{2,1,0:T(8,128)(2,1)S(1)}, u32[]{:S(2)}, u32[]{:S(2)}) collective-permute-start(bf16[1,15,1024]{2,1,0:T(8,128)(2,1)S(1)} %get-tuple-element.100), channel_id=1, source_target_pairs={{1,0},{2,1},{3,2},{4,3},{5,4},{6,5},{7,6},{8,7},{9,8},{10,9},{11,1... | collective-permute-start | bytes 92168 | tf_op jit(solution)/shard_map/ppermute | solution.py:26
  121.6 10.6 %copy-start.12 = (f32[1,1024]{1,0:T(1,128)S(1)}, f32[1,1024]{1,0:T(1,128)}, u32[]{:S(2)}) copy-start(f32[1,1024]{1,0:T(1,128)} %copy-done.11) | copy-start | bytes 12292
  121.6 10.6 %copy-start.14 = (f32[1,1024]{1,0:T(1,128)S(1)}, f32[1,1024]{1,0:T(1,128)}, u32[]{:S(2)}) copy-start(f32[1,1024]{1,0:T(1,128)} %copy-done.13) | copy-start | bytes 12292
  121.6 10.6 %copy-start.16 = (f32[1,1024]{1,0:T(1,128)S(1)}, f32[1,1024]{1,0:T(1,128)}, u32[]{:S(2)}) copy-start(f32[1,1024]{1,0:T(1,128)} %copy-done.15) | copy-start | bytes 12292
  121.8 13.5 %copy-start.1 = (bf16[1024,2048]{1,0:T(8,128)(2,1)S(1)}, bf16[1024,2048]{1,0:T(8,128)(2,1)}, u32[]{:S(2)}) copy-start(bf16[1024,2048]{1,0:T(8,128)(2,1)} %all-gather.2.cloned.1.call-done) | copy-start | bytes 12582916
  121.8 13.5 %copy-start.42 = (f32[1024]{0:T(1024)S(1)}, f32[1024]{0:T(1024)}, u32[]{:S(2)}) copy-start(f32[1024]{0:T(1024)} %param.20) | copy-start | bytes 12292
  121.8 13.5 %copy-start.44 = (f32[128]{0:T(128)S(1)}, f32[128]{0:T(128)}, u32[]{:S(2)}) copy-start(f32[128]{0:T(128)} %copy-done.43) | copy-start | bytes 1540
  121.8 13.5 %copy-start.46 = (f32[128]{0:T(128)S(1)}, f32[128]{0:T(128)}, u32[]{:S(2)}) copy-start(f32[128]{0:T(128)} %copy-done.45) | copy-start | bytes 1540
  123.8 11.5 %copy-start.3 = (f32[128,1024]{1,0:T(8,128)S(1)}, f32[128,1024]{1,0:T(8,128)}, u32[]{:S(2)}) copy-start(f32[128,1024]{1,0:T(8,128)} %copy-done.2) | copy-start | bytes 1572868
  123.8 7.3 %collective-permute-start.2 = (bf16[1,15,1024]{2,1,0:T(8,128)(2,1)S(1)}, bf16[1,15,1024]{2,1,0:T(8,128)(2,1)S(1)}, u32[]{:S(2)}, u32[]{:S(2)}) collective-permute-start(bf16[1,15,1024]{2,1,0:T(8,128)(2,1)S(1)} %get-tuple-element.98), channel_id=1, source_target_pairs={{1,0},{2,1},{3,2},{4,3},{5,4},{6,5},{7,6},{8,7},{9,8},{10,9},{11,1... | collective-permute-start | bytes 92168 | tf_op jit(solution)/shard_map/ppermute | solution.py:26
  126.4 5.9 %collective-permute-start.3 = (bf16[1,15,1024]{2,1,0:T(8,128)(2,1)S(1)}, bf16[1,15,1024]{2,1,0:T(8,128)(2,1)S(1)}, u32[]{:S(2)}, u32[]{:S(2)}) collective-permute-start(bf16[1,15,1024]{2,1,0:T(8,128)(2,1)S(1)} %get-tuple-element.99), channel_id=1, source_target_pairs={{0,1},{1,2},{2,3},{3,4},{4,5},{5,6},{6,7},{7,8},{8,9},{9,10},{10,1... | collective-permute-start | bytes 92168 | tf_op jit(solution)/shard_map/ppermute | solution.py:24
  137.9 70.4 %copy-start.47 = (f32[1024]{0:T(1024)S(1)}, f32[1024]{0:T(1024)}, u32[]{:S(2)}) copy-start(f32[1024]{0:T(1024)} %get-tuple-element.76) | copy-start | bytes 12292
  137.9 70.4 %copy-start.48 = (f32[1024]{0:T(1024)S(1)}, f32[1024]{0:T(1024)}, u32[]{:S(2)}) copy-start(f32[1024]{0:T(1024)} %get-tuple-element.77) | copy-start | bytes 12292
  137.9 70.4 %copy-start.49 = (f32[1024]{0:T(1024)S(1)}, f32[1024]{0:T(1024)}, u32[]{:S(2)}) copy-start(f32[1024]{0:T(1024)} %get-tuple-element.78) | copy-start | bytes 12292
  137.9 70.4 %copy-start.50 = (f32[1024]{0:T(1024)S(1)}, f32[1024]{0:T(1024)}, u32[]{:S(2)}) copy-start(f32[1024]{0:T(1024)} %get-tuple-element.79) | copy-start | bytes 12292
  139.7 68.6 %copy-start.51 = (f32[1024]{0:T(1024)S(1)}, f32[1024]{0:T(1024)}, u32[]{:S(2)}) copy-start(f32[1024]{0:T(1024)} %get-tuple-element.80) | copy-start | bytes 12292
  139.7 68.6 %copy-start.52 = (f32[1024]{0:T(1024)S(1)}, f32[1024]{0:T(1024)}, u32[]{:S(2)}) copy-start(f32[1024]{0:T(1024)} %get-tuple-element.81) | copy-start | bytes 12292
  139.7 104.3 %all-reduce.3.cloned.1.call-start = ((), (), s32[]{:S(2)}) async-start(), calls=%async_computation.7 | async-start | bytes 131072 | tf_op jit(solution)/shard_map/psum | solution.py:195
  208.0 162.9 %all-reduce.5.cloned.1.call-start = ((), (), s32[]{:S(2)}) async-start(), calls=%async_computation.8 | async-start | bytes 262144 | tf_op jit(solution)/shard_map/psum | solution.py:170
  (17 other events, 139.5 us)
Sparse Core Ops, SparseCore 0:
  10.7 95.3 all-gather.1
  139.9 66.5 reduce-scatter.1
  209.3 34.6 all-reduce.2
  250.0 120.8 all-reduce.4
where the time goes:
time: 383 us; the launch traced here: 379 us
  waiting for transfers between devices  269 us (70%)
  starting transfers between devices  41.6 us (11%)
  other arithmetic  20.7 us (5%)
  matrix products  17.4 us (5%)
  local copies, waits for them, and re-layouts  16.1 us (4%)
  between operations  14.7 us (4%)
    psum x1, waiting for transfers between devices, body(): grad_kernel = lax.psum(kernel_terms(padded, grad_conv, rows), ('dp', 'seq'))  125 us
    reduce_scatter x1, waiting for transfers between devices, body(): lax.psum_scatter(lax.dot_general(attended, grad_mid, (((0,), (0,)), ((),...  57 us
    psum x1, waiting for transfers between devices, body(): lax.psum(partial_rows.astype(jnp.bfloat16), 'dp').astype(jnp.float32)  30.7 us
    all_gather x1, waiting for transfers between devices, body(): lax.all_gather(conv_in, 'seq', axis=1, tiled=True)  21.6 us
    all_to_all x1, starting transfers between devices, body(): lax.all_to_all(attended_heads.reshape(1, batch, seq_count, part, DH), 'se...  10.4 us
    all_to_all x1, waiting for transfers between devices, body(): lax.all_to_all(attended_heads.reshape(1, batch, seq_count, part, DH), 'se...  10.3 us
    reduce_sum x4, other arithmetic, kernel_terms(): terms.append(jnp.sum(product, axis=(0, 1)))  9.87 us
    all_to_all x1, waiting for transfers between devices, body(): lax.all_to_all(value_send, 'seq', split_axis=0, concat_axis=2, tiled=True)  9.2 us
  transfers between devices with their start and end apart: 12, of which 10 were waited for; matrix products, arithmetic and copies ran while one was open for 9% of the time, Pallas kernels for 0%

commit v1 on v0

v1 whole, which is shorter than its diff:
```python
import functools

import jax
import jax.numpy as jnp
from jax import lax
from jax.experimental import pallas as pl
from jax.experimental.pallas import tpu as pltpu
from jax.sharding import PartitionSpec as P

HEADS = 8
DH = 64
KW = 31
EPS = 1e-05
F32 = jnp.float32
BF16 = jnp.bfloat16
MESH = pl.DeviceIdType.MESH


def sigmoid(x):
    return 1.0 / (1.0 + jnp.exp(-x))


def toggled(me, r):
    out = me
    b = 1
    while b <= r:
        if r & b:
            out = out + b * (1 - 2 * ((me // b) % 2))
        b *= 2
    return out


def kernel(
    S, DPN,
    q_ref, k_ref, v_ref, res_ref, op_ref, ci_ref, co_ref, dk_ref, ng_ref, ct_ref,
    lo_ref, gm_ref, go_ref, gk_ref,
    kvs, kvr, qs, qr, ats, atr, wf,
    att_ref, mid_ref, val_ref, gate_ref, gact_ref, act_ref, gcb_ref, gp, cp, gproj_ref,
    halo_s, halo_r, dkf,
    gkl, gk1s, gk1r, gk2s, gk2r, gk3r,
    gods, godr, gos, gor, gofr,
    kv_ss, kv_rs, q_ss, q_rs, at_ss, at_rs, w_ss, w_rs, sb_ss, sb_rs,
    h_ss, h_rs, k1_ss, k1_rs, k2_ss, k2_rs, k3_ss, k3_rs,
    gd_ss, gd_rs, g_ss, g_rs, gf_ss, gf_rs,
):
    me = lax.axis_index("seq")
    dp = lax.axis_index("dp")
    rows, model = res_ref.shape
    group = S // HEADS
    part = rows // group
    cw = ci_ref.shape[1]
    bits = []
    b = S // 2
    while b >= 1:
        bits.append(b)
        b //= 2
    order_a = bits
    order_b = bits[:-2] + [bits[-1], bits[-2]]

    def rc(src, dst, ss, rs, seq_id, dp_id):
        return pltpu.make_async_remote_copy(
            src_ref=src, dst_ref=dst, send_sem=ss, recv_sem=rs,
            device_id=(dp_id, seq_id), device_id_type=MESH,
        )

    def peers(fn, n, mine):
        def step(i, c):
            fn(lax.rem(mine + i, n))
            return c
        lax.fori_loop(1, n, step, 0)

    barrier = pltpu.get_barrier_semaphore()

    def hello_seq(j):
        pl.semaphore_signal(barrier, inc=1, device_id=(dp, j), device_id_type=MESH)

    def hello_dp(j):
        pl.semaphore_signal(barrier, inc=1, device_id=(j, me), device_id_type=MESH)

    peers(hello_seq, S, me)
    peers(hello_dp, DPN, dp)

    zeros64 = jnp.zeros((part, DH), BF16)
    for h in range(HEADS):
        cols = slice(h * DH, (h + 1) * DH)
        kvs[h] = jnp.concatenate([k_ref[:, cols], v_ref[:, cols]], axis=1)
        for g in range(group):
            piece = q_ref[g * part:(g + 1) * part, cols] * jnp.asarray(DH ** -0.5, BF16)
            qs[h * group + g] = jnp.concatenate([piece, zeros64], axis=1)
    wf[me] = ci_ref[...]
    pl.semaphore_wait(barrier, S - 1 + DPN - 1)

    def kv_copy(j, src):
        return rc(kvs.at[j // group], kvr.at[src], kv_ss.at[j], kv_rs.at[src], j, dp)

    def q_copy(j, src):
        return rc(qs.at[j], qr.at[src], q_ss.at[j], q_rs.at[src], j, dp)

    def send_qkv(j):
        kv_copy(j, me).start()
        q_copy(j, me).start()

    peers(send_qkv, S, me)
    kvr[me] = kvs[me // group]
    qr[me] = qs[me]

    share = 2 if DPN % 2 == 0 else 1
    core = lax.rem(dp, share)
    sib = dp + 1 - 2 * core
    half = model // share
    sub = half // 2

    def w_copy(o, r, b):
        chunk = toggled(me, r)
        begin = pl.multiple_of(core * half + o * sub, sub)
        where = wf.at[chunk, pl.ds(begin, sub)]
        return rc(where, where, w_ss.at[o, r + b], w_rs.at[o, r + b], toggled(me, b), dp)

    def sib_copy(r):
        where = wf.at[toggled(me, r), pl.ds(pl.multiple_of(core * half, half), half)]
        return rc(where, where, sb_ss.at[r], sb_rs.at[r], me, sib)

    def sib_recv(r):
        where = wf.at[toggled(me, r), pl.ds(pl.multiple_of((1 - core) * half, half), half)]
        return rc(where, where, sb_ss.at[r], sb_rs.at[r], me, sib)

    def subsets(order, n):
        out = [0]
        for b in order[:n]:
            out = out + [r + b for r in out]
        return out

    def w_recv_wait(o, r, b):
        chunk = toggled(me, r + b)
        begin = pl.multiple_of(core * half + o * sub, sub)
        where = wf.at[chunk, pl.ds(begin, sub)]
        rc(where, where, w_ss.at[o, r + b], w_rs.at[o, r + b], toggled(me, b), dp).wait_recv()

    done = set()

    def gather_step(n):
        for o, order in enumerate((order_a, order_b)):
            if n > 0:
                for r in subsets(order, n - 1):
                    w_recv_wait(o, r, order[n - 1])
            if n < len(bits):
                for r in subsets(order, n):
                    w_copy(o, r, order[n]).start()
        if share == 2:
            both = set(subsets(order_a, n)) & set(subsets(order_b, n))
            for r in sorted(both - done - {0}):
                sib_copy(r).start()
                done.add(r)

    gather_step(0)

    def wait_qkv(j):
        kv_copy(j, j).wait_recv()
        q_copy(j, j).wait_recv()

    peers(wait_qkv, S, me)
    gather_step(1)

    owners = max(1, 256 // part)
    blocks = S // owners
    kv = kvr[...].reshape(S * rows, 2 * DH)

    def at_copy(j, src):
        return rc(ats.at[j], atr.at[src], at_ss.at[j], at_rs.at[src], j, dp)

    def attend(i, c):
        first = i * owners
        q = qr[pl.ds(first, owners)].reshape(owners * part, 2 * DH)
        s = lax.dot_general(q, kv, (((1,), (1,)), ((), ())), preferred_element_type=F32)
        top = jnp.max(s, axis=1, keepdims=True)
        e = jnp.exp(s - top)
        total = jnp.sum(e, axis=1, keepdims=True)
        mixed = jnp.dot(e.astype(BF16), kv, preferred_element_type=F32)
        out = (mixed / total).astype(BF16).reshape(owners, part, 2 * DH)
        ats[pl.ds(first, owners)] = out

        def send(n, c2):
            j = first + n

            @pl.when(j != me)
            def _():
                at_copy(j, me).start()
            return c2
        lax.fori_loop(0, owners, send, 0)
        return c

    lax.fori_loop(0, blocks // 2, attend, 0)
    gather_step(2)
    lax.fori_loop(blocks // 2, blocks, attend, 0)
    for n in range(3, len(bits)):
        gather_step(n)
    atr[me] = ats[me]
    dkf[0:KW] = dk_ref[...].astype(F32)

    ct = ct_ref[...]
    gact_ref[...] = lax.dot_general(
        ct, co_ref[...], (((1,), (1,)), ((), ())), preferred_element_type=F32
    )

    def wait_at(j):
        at_copy(j, j).wait_recv()

    peers(wait_at, S, me)
    for g in range(group):
        for h in range(0, HEADS, 2):
            left = atr[h * group + g][:, DH:]
            right = atr[(h + 1) * group + g][:, DH:]
            att_ref[g * part:(g + 1) * part, h * DH:(h + 2) * DH] = jnp.concatenate(
                [left, right], axis=1
            )
    mid = (
        res_ref[...].astype(F32)
        + jnp.dot(att_ref[...], op_ref[...], preferred_element_type=F32)
    ).astype(BF16)
    mid_ref[...] = mid
    wide = mid.astype(F32)
    centered = wide - jnp.mean(wide, axis=1, keepdims=True)
    rscale = lax.rsqrt(jnp.mean(centered * centered, axis=1, keepdims=True) + EPS)
    gain = ng_ref[...]
    normed = (centered * rscale * gain).astype(BF16)

    gather_step(len(bits))
    if share == 2:
        for r in range(1, S):
            sib_recv(r).wait_recv()

    per = max(1, 256 // cw)
    wide_cols = per * cw

    def weights(n):
        return jnp.concatenate([wf[n * per + i] for i in range(per)], axis=1)

    count = model // wide_cols
    for n in range(count):
        cols = slice(n * wide_cols, (n + 1) * wide_cols)
        value = jnp.dot(normed, weights(n), preferred_element_type=F32)
        gate = sigmoid(jnp.dot(normed, weights(count + n), preferred_element_type=F32))
        val_ref[:, cols] = value
        gate_ref[:, cols] = gate
        gated = (value * gate).astype(BF16)
        gp[16:16 + rows, cols] = gated.astype(F32)
        halo_s[0, :, cols] = gated[:16]
        halo_s[1, :, cols] = gated[rows - 16:]

    def halo(base, act):
        def left_send():
            return rc(halo_s.at[base], halo_r.at[base + 1], h_ss.at[base], h_rs.at[base + 1],
                      lax.rem(me + S - 1, S), dp)

        def right_send():
            return rc(halo_s.at[base + 1], halo_r.at[base], h_ss.at[base + 1], h_rs.at[base],
                      lax.rem(me + 1, S), dp)

        @pl.when(me > 0)
        def _():
            if act == "start":
                left_send().start()
            elif act == "wait":
                rc(halo_s.at[base + 1], halo_r.at[base], h_ss.at[base + 1], h_rs.at[base],
                   lax.rem(me + S - 1, S), dp).wait_recv()
            else:
                left_send().wait_send()

        @pl.when(me < S - 1)
        def _():
            if act == "start":
                right_send().start()
            elif act == "wait":
                rc(halo_s.at[base], halo_r.at[base + 1], h_ss.at[base], h_rs.at[base + 1],
                   lax.rem(me + 1, S), dp).wait_recv()
            else:
                right_send().wait_send()

    def place(base, buf):
        @pl.when(me > 0)
        def _():
            buf[0:16] = halo_r[base].astype(F32)

        @pl.when(me == 0)
        def _():
            buf[0:16] = jnp.zeros((16, model), F32)

        @pl.when(me < S - 1)
        def _():
            buf[16 + rows:32 + rows] = halo_r[base + 1].astype(F32)

        @pl.when(me == S - 1)
        def _():
            buf[16 + rows:32 + rows] = jnp.zeros((16, model), F32)

    halo(0, "start")
    halo(0, "wait")
    place(0, gp)

    LB = 128

    def forward_block(n, c):
        cols = pl.ds(pl.multiple_of(n * LB, LB), LB)
        acc = jnp.zeros((rows, LB), F32)
        for k in range(KW):
            acc = acc + dkf[k:k + 1, cols] * gp[k + 1:k + 1 + rows, cols]
        sg = sigmoid(acc)
        act_ref[:, cols] = (acc * sg).astype(BF16)
        gc = (gact_ref[:, cols] * sg * (1.0 + acc * (1.0 - sg))).astype(BF16)
        cp[16:16 + rows, cols] = gc.astype(F32)
        halo_s[2, :, cols] = gc[:16]
        halo_s[3, :, cols] = gc[rows - 16:]
        return c

    lax.fori_loop(0, model // LB, forward_block, 0)
    halo(2, "start")

    def kernel_block(n, c):
        cols = pl.ds(pl.multiple_of(n * LB, LB), LB)
        gc = cp[16:16 + rows, cols]
        for k in range(KW):
            gkl[k:k + 1, cols] = jnp.sum(
                gp[k + 1:k + 1 + rows, cols] * gc, axis=0, keepdims=True
            )
        gkl[KW:KW + 1, cols] = jnp.zeros((1, LB), F32)
        return c

    lax.fori_loop(0, model // LB, kernel_block, 0)

    kc = gk1s.shape[2]
    across = model // kc
    for j in range(S):
        r0, c0 = (j // across) * 8, (j % across) * kc
        gk1s[j] = gkl[r0:r0 + 8, c0:c0 + kc]

    def k1(j, src):
        return rc(gk1s.at[j], gk1r.at[src], k1_ss.at[j], k1_rs.at[src], j, dp)

    peers(lambda j: k1(j, me).start(), S, me)
    gk1r[me] = gk1s[me]

    lo_ref[...] = (
        mid_ref[...].astype(F32)
        + jnp.dot(act_ref[...], co_ref[...], preferred_element_type=F32)
    ).astype(BF16)

    halo(2, "wait")
    place(2, cp)

    peers(lambda j: k1(j, j).wait_recv(), S, me)
    gk2s[...] = jnp.sum(gk1r[...], axis=0)

    def k2(j, src):
        return rc(gk2s, gk2r.at[src], k2_ss.at[j], k2_rs.at[src], me, j)

    peers(lambda j: k2(j, dp).start(), DPN, dp)
    gk2r[dp] = gk2s[...]

    def backward_block(n, c):
        cols = pl.ds(pl.multiple_of(n * LB, LB), LB)
        acc = jnp.zeros((rows, LB), F32)
        for k in range(KW):
            acc = acc + dkf[k:k + 1, cols] * cp[31 - k:31 - k + rows, cols]
        gate = gate_ref[:, cols]
        first = acc * gate
        gproj_ref[:, cols] = first.astype(BF16)
        gproj_ref[:, pl.ds(pl.multiple_of(model + n * LB, LB), LB)] = (
            first * val_ref[:, cols] * (1.0 - gate)
        ).astype(BF16)
        return c

    lax.fori_loop(0, model // LB, backward_block, 0)

    peers(lambda j: k2(j, j).wait_recv(), DPN, dp)
    gk3r[me] = jnp.sum(gk2r[...], axis=0)

    def k3(j, src):
        return rc(gk3r.at[src], gk3r.at[src], k3_ss.at[j], k3_rs.at[src], j, dp)

    peers(lambda j: k3(j, me).start(), S, me)

    gn = jnp.zeros((rows, model), F32)
    for n in range(2 * count):
        gn = gn + lax.dot_general(
            gproj_ref[:, n * wide_cols:(n + 1) * wide_cols], weights(n),
            (((1,), (1,)), ((), ())), preferred_element_type=F32,
        )
    wide = mid_ref[...].astype(F32)
    centered = wide - jnp.mean(wide, axis=1, keepdims=True)
    rscale = lax.rsqrt(jnp.mean(centered * centered, axis=1, keepdims=True) + EPS)
    hat = centered * rscale
    dh = gn * ng_ref[...]
    inner = (
        dh
        - jnp.mean(dh, axis=1, keepdims=True)
        - hat * jnp.mean(dh * hat, axis=1, keepdims=True)
    )
    gm = (ct_ref[...].astype(F32) + rscale * inner).astype(BF16)
    gm_ref[...] = gm

    att_t = att_ref[...].T
    nc = model // DPN
    orow = go_ref.shape[0]
    for d in range(DPN):
        piece = jnp.dot(att_t, gm[:, d * nc:(d + 1) * nc], preferred_element_type=F32)
        gods[d] = piece.astype(BF16).reshape(S, orow, nc)

    def gd(j, src):
        return rc(gods.at[j], godr.at[src], gd_ss.at[j], gd_rs.at[src], me, j)

    peers(lambda j: gd(j, dp).start(), DPN, dp)
    godr[dp] = gods[dp]
    peers(lambda j: gd(j, j).wait_recv(), DPN, dp)

    def sum_dp(j, c):
        acc = godr[0, j].astype(F32)
        for d in range(1, DPN):
            acc = acc + godr[d, j].astype(F32)
        gos[j] = acc.astype(BF16)
        return c

    lax.fori_loop(0, S, sum_dp, 0)

    def go(j, src):
        return rc(gos.at[j], gor.at[src], g_ss.at[j], g_rs.at[src], j, dp)

    peers(lambda j: go(j, me).start(), S, me)
    gor[me] = gos[me]

    peers(lambda j: k3(j, j).wait_recv(), S, me)
    for j in range(S):
        r0, c0 = (j // across) * 8, (j % across) * kc
        n = min(8, KW - r0)
        gk_ref[r0:r0 + n, c0:c0 + kc] = gk3r[j][:n]

    peers(lambda j: go(j, j).wait_recv(), S, me)
    acc = gor[0].astype(F32)
    for j in range(1, S):
        acc = acc + gor[j].astype(F32)
    gofr[dp] = acc

    def gf(j, src):
        return rc(gofr.at[src], gofr.at[src], gf_ss.at[j], gf_rs.at[src], me, j)

    peers(lambda j: gf(j, dp).start(), DPN, dp)

    def close(j):
        kv_copy(j, me).wait_send()
        q_copy(j, me).wait_send()
        at_copy(j, me).wait_send()
        k1(j, me).wait_send()
        k3(j, me).wait_send()
        go(j, me).wait_send()

    peers(close, S, me)
    for o, order in enumerate((order_a, order_b)):
        for n in range(len(bits)):
            for r in subsets(order, n):
                w_copy(o, r, order[n]).wait_send()
    if share == 2:
        for r in range(1, S):
            sib_copy(r).wait_send()
    halo(0, "close")
    halo(2, "close")

    peers(lambda j: gf(j, j).wait_recv(), DPN, dp)
    for d in range(DPN):
        go_ref[:, d * nc:(d + 1) * nc] = gofr[d]

    def close_dp(j):
        k2(j, dp).wait_send()
        gd(j, dp).wait_send()
        gf(j, dp).wait_send()

    peers(close_dp, DPN, dp)


def body(queries, keys, values, residual, out_proj, conv_in, conv_out, depth_kernel, norm_gain,
         cotangent):
    S = lax.axis_size("seq")
    DPN = lax.axis_size("dp")
    batch, rows, width = queries.shape
    model = residual.shape[2]
    group = S // HEADS
    part = rows // group
    cw = conv_in.shape[1]
    kc = 32 * model // (8 * S)
    orow = width // S
    nc = model // DPN
    V = pltpu.VMEM
    D = pltpu.SemaphoreType.DMA
    wide = V((rows, model), F32)
    slim = V((rows, model), BF16)
    scratch = [
        V((HEADS, rows, 2 * DH), BF16), V((S, rows, 2 * DH), BF16),
        V((S, part, 2 * DH), BF16), V((S, part, 2 * DH), BF16),
        V((S, part, 2 * DH), BF16), V((S, part, 2 * DH), BF16),
        V((S, model, cw), BF16),
        V((rows, width), BF16), slim, wide, wide, wide, slim, slim,
        V((rows + 32, model), F32), V((rows + 32, model), F32), V((rows, 2 * model), BF16),
        V((4, 16, model), BF16), V((4, 16, model), BF16), V((32, model), F32),
        V((32, model), F32), V((S, 8, kc), F32), V((S, 8, kc), F32),
        V((8, kc), F32), V((DPN, 8, kc), F32), V((S, 8, kc), F32),
        V((DPN, S, orow, nc), BF16), V((DPN, S, orow, nc), BF16),
        V((S, orow, nc), BF16), V((S, orow, nc), BF16), V((DPN, orow, nc), F32),
        D((S,)), D((S,)), D((S,)), D((S,)), D((S,)), D((S,)), D((2, S)), D((2, S)), D((S,)), D((S,)),
        D((4,)), D((4,)), D((S,)), D((S,)), D((DPN,)), D((DPN,)), D((S,)), D((S,)),
        D((DPN,)), D((DPN,)), D((S,)), D((S,)), D((DPN,)), D((DPN,)),
    ]
    vm = pl.BlockSpec(memory_space=pltpu.VMEM)
    lo, gm, go, gk = pl.pallas_call(
        functools.partial(kernel, S, DPN),
        out_shape=[
            jax.ShapeDtypeStruct((rows, model), BF16),
            jax.ShapeDtypeStruct((rows, model), BF16),
            jax.ShapeDtypeStruct((orow, model), F32),
            jax.ShapeDtypeStruct((KW, model), F32),
        ],
        in_specs=[vm] * 10,
        out_specs=[vm] * 4,
        scratch_shapes=scratch,
        compiler_params=pltpu.CompilerParams(
            collective_id=0, has_side_effects=True, vmem_limit_bytes=60 * 1024 * 1024
        ),
    )(
        queries[0], keys[0], values[0], residual[0], out_proj, conv_in, conv_out, depth_kernel,
        norm_gain.reshape(1, model), cotangent[0],
    )
    return lo[None], gm[None], go, gk


def solution(mesh):
    return jax.shard_map(
        body,
        mesh=mesh,
        in_specs=(
            P("dp", "seq", None),
            P("dp", "seq", None),
            P("dp", "seq", None),
            P("dp", "seq", None),
            P(),
            P(None, "seq"),
            P(),
            P(),
            P(),
            P("dp", "seq", None),
        ),
        out_specs=(P("dp", "seq", None), P("dp", "seq", None), P("seq", None), P()),
        check_vma=False,
    )
```

time: 383 us -> 109 us (0.28); the launches traced: 379 us -> 109 us
  waiting for transfers between devices: 269 us -> 0 us
  Pallas kernels: 0 us -> 102 us
  starting transfers between devices: 41.6 us -> 0 us
  other arithmetic: 20.7 us -> 0 us
  matrix products: 17.4 us -> 0 us
  between operations: 14.7 us -> 0.64 us
  local copies, waits for them, and re-layouts: 16.1 us -> 6.47 us
    psum x2 -> x0, waiting for transfers between devices: 156 us -> none  [the longest x1 125 us: body(): grad_kernel = lax.psum(kernel_terms(padded, grad_conv, rows), ('dp', 'seq'))]
    pallas_call x0 -> x1, Pallas kernels: none -> 102 us  [body(): pl.pallas_call(functools.partial(kernel, S, DPN), out_shape=[jax.ShapeDty...]
    reduce_scatter x1 -> x0, waiting for transfers between devices: 57 us -> none  [body(): lax.psum_scatter(lax.dot_general(attended, grad_mid, (((0,), (0,)), ((),...]
    all_to_all x4 -> x0, waiting for transfers between devices: 28.9 us -> none  [the longest x1 10.3 us: body(): lax.all_to_all(attended_heads.reshape(1, batch, seq_count, part, DH), 'se...]
    all_to_all x4 -> x0, starting transfers between devices: 28.1 us -> none  [the longest x1 10.4 us: body(): lax.all_to_all(attended_heads.reshape(1, batch, seq_count, part, DH), 'se...]
    all_gather x1 -> x0, waiting for transfers between devices: 21.6 us -> none  [body(): lax.all_gather(conv_in, 'seq', axis=1, tiled=True)]
    dot_general x10 -> x0, matrix products: 17.4 us -> none  [the longest x2 3.21 us: one_block(): mixed = jnp.dot(weights, value_rows, preferred_element_type=jnp.float32)]
    ppermute x4 -> x0, starting transfers between devices: 13.4 us -> none  [the longest x2 6.83 us: padded_2(): lax.ppermute(tail, axis, [(i, (i + 1) % count) for i in range(ends)])]
  transfers between devices with their start and end apart: 12 -> 0, of which waited for: 10 -> 0; matrix products, arithmetic and copies ran while one was open for 9% -> 0% of each run, Pallas kernels for 0% -> 0%
where the time goes in v1:
time: 109 us
  Pallas kernels  102 us (94%)
  local copies, waits for them, and re-layouts  6.47 us (6%)
    pallas_call x1, Pallas kernels, body(): pl.pallas_call(functools.partial(kernel, S, DPN), out_shape=[jax.ShapeDty...  102 us
    unnamed x4, local copies, waits for them, and re-layouts  6.47 us

profile of v1, /device:TPU:13, one launch (start us, length us, event | category | flops | bytes accessed | tf_op | source)
XLA Modules:
  0.0 109.2 jit_solution(12305626046725306220)
XLA Ops:
  0.6 102.1 %shard_map.129 = (bf16[128,1024]{1,0:T(8,128)(2,1)}, bf16[128,1024]{1,0:T(8,128)(2,1)}, f32[32,1024]{1,0:T(8,128)}, f32[31,1024]{1,0:T(8,128)}) custom-call(bf16[128,512]{1,0:T(8,128)(2,1)} %bitcast.12, bf16[128,512]{1,0:T(8,128)(2,1)} %bitcast.13, bf16[128,512]{1,0:T(8,128)(2,1)} %bitcast.14, bf16[128,1024]{1,0:T(8,128)(2,1)} %bitcast.8, ...), custom_call_target="tpu_custom_call" | custom-call | tf_op jit(solution)/shard_map/pallas_call | solution.py:511
  102.8 1.7 %copy.18 = bf16[1,128,1024]{2,1,0:T(8,128)(2,1)} copy(bf16[1,128,1024]{2,1,0:T(8,128)(2,1)} %bitcast.11) | data formatting | bytes 524288
  104.4 1.7 %copy.19 = bf16[1,128,1024]{2,1,0:T(8,128)(2,1)} copy(bf16[1,128,1024]{2,1,0:T(8,128)(2,1)} %bitcast.10) | data formatting | bytes 524288
  106.1 1.6 %copy.20 = f32[32,1024]{1,0:T(8,128)} copy(f32[32,1024]{1,0:T(8,128)} %get-tuple-element.18) | data formatting | bytes 262144
  107.7 1.6 %copy.21 = f32[31,1024]{1,0:T(8,128)} copy(f32[31,1024]{1,0:T(8,128)} %get-tuple-element.19) | data formatting | bytes 253952

commit v2 on v1

--- a/solution.py
+++ b/solution.py
@@ -32,8 +32,10 @@
 
 def kernel(
     S, DPN,
-    q_ref, k_ref, v_ref, res_ref, op_ref, ci_ref, co_ref, dk_ref, ng_ref, ct_ref,
-    lo_ref, gm_ref, go_ref, gk_ref,
+    q_in, k_in, v_in, res_in, op_in, ci_in, co_in, dk_in, ng_in, ct_in,
+    lo_out, gm_out, go_out, gk_out,
+    q_ref, k_ref, v_ref, res_ref, op_ref, co_ref, dk_ref, ng_ref, ct_ref,
+    lo_ref, gm_ref, go_ref, gk_ref, in_sem, out_sem, fw_ss,
     kvs, kvr, qs, qr, ats, atr, wf,
     att_ref, mid_ref, val_ref, gate_ref, gact_ref, act_ref, gcb_ref, gp, cp, gproj_ref,
     halo_s, halo_r, dkf,
@@ -45,17 +47,39 @@
 ):
     me = lax.axis_index("seq")
     dp = lax.axis_index("dp")
-    rows, model = res_ref.shape
+    rows, model = res_in.shape
     group = S // HEADS
     part = rows // group
-    cw = ci_ref.shape[1]
+    cw = ci_in.shape[1]
+    member = lax.rem(me, group)
+    lead = me - member
+
+    loads = [
+        pltpu.make_async_copy(src, dst, in_sem.at[n])
+        for n, (src, dst) in enumerate([
+            (q_in, q_ref), (k_in, k_ref), (v_in, v_ref), (ci_in, wf.at[me]), (ct_in, ct_ref),
+            (co_in, co_ref), (op_in, op_ref), (res_in, res_ref), (ng_in, ng_ref),
+            (dk_in, dk_ref),
+        ])
+    ]
+    for load in loads:
+        load.start()
+    stores = [
+        pltpu.make_async_copy(src, dst, out_sem.at[n])
+        for n, (src, dst) in enumerate([
+            (lo_ref, lo_out), (gm_ref, gm_out), (go_ref, go_out), (gk_ref, gk_out),
+        ])
+    ]
     bits = []
     b = S // 2
     while b >= 1:
         bits.append(b)
         b //= 2
-    order_a = bits
-    order_b = bits[:-2] + [bits[-1], bits[-2]]
+    swapped = bits[:-2] + [bits[-1], bits[-2]]
+    back = [bits[-1], bits[-2]] + bits[:-2]
+    turned = [bits[-2], bits[-1]] + bits[:-2]
+    orders = [bits, bits, bits, swapped, swapped, swapped, back, turned]
+    pieces = len(orders)
 
     def rc(src, dst, ss, rs, seq_id, dp_id):
         return pltpu.make_async_remote_copy(
@@ -79,6 +103,9 @@
 
     peers(hello_seq, S, me)
     peers(hello_dp, DPN, dp)
+
+    for load in loads[:3]:
+        load.wait()
 
     zeros64 = jnp.zeros((part, DH), BF16)
     for h in range(HEADS):
@@ -87,28 +114,37 @@
         for g in range(group):
             piece = q_ref[g * part:(g + 1) * part, cols] * jnp.asarray(DH ** -0.5, BF16)
             qs[h * group + g] = jnp.concatenate([piece, zeros64], axis=1)
-    wf[me] = ci_ref[...]
     pl.semaphore_wait(barrier, S - 1 + DPN - 1)
 
-    def kv_copy(j, src):
-        return rc(kvs.at[j // group], kvr.at[src], kv_ss.at[j], kv_rs.at[src], j, dp)
+    def kv_copy(h):
+        return rc(kvs.at[h], kvr.at[me], kv_ss.at[h], kv_rs.at[me], h * group + member, dp)
+
+    def kv_hand(src, i, e):
+        where = kvr.at[src]
+        return rc(where, where, fw_ss.at[i, e], kv_rs.at[src],
+                  lead + lax.rem(member + e, group), dp)
+
+    def kv_wait(src, peer):
+        where = kvr.at[src]
+        rc(where, where, kv_ss.at[0], kv_rs.at[src], peer, dp).wait_recv()
 
     def q_copy(j, src):
         return rc(qs.at[j], qr.at[src], q_ss.at[j], q_rs.at[src], j, dp)
 
-    def send_qkv(j):
-        kv_copy(j, me).start()
-        q_copy(j, me).start()
-
-    peers(send_qkv, S, me)
-    kvr[me] = kvs[me // group]
+    mine = me // group
+    peers(lambda h: kv_copy(h).start(), HEADS, mine)
+    peers(lambda j: q_copy(j, me).start(), S, me)
+    kvr[me] = kvs[mine]
     qr[me] = qs[me]
+    for e in range(1, group):
+        kv_hand(me, 0, e).start()
+    loads[3].wait()
 
     share = 2 if DPN % 2 == 0 else 1
     core = lax.rem(dp, share)
     sib = dp + 1 - 2 * core
     half = model // share
-    sub = half // 2
+    sub = half // pieces
 
     def w_copy(o, r, b):
         chunk = toggled(me, r)
@@ -139,7 +175,7 @@
     done = set()
 
     def gather_step(n):
-        for o, order in enumerate((order_a, order_b)):
+        for o, order in enumerate(orders):
             if n > 0:
                 for r in subsets(order, n - 1):
                     w_recv_wait(o, r, order[n - 1])
@@ -147,18 +183,30 @@
                 for r in subsets(order, n):
                     w_copy(o, r, order[n]).start()
         if share == 2:
-            both = set(subsets(order_a, n)) & set(subsets(order_b, n))
+            both = set.intersection(*[set(subsets(order, n)) for order in orders])
             for r in sorted(both - done - {0}):
                 sib_copy(r).start()
                 done.add(r)
 
     gather_step(0)
 
-    def wait_qkv(j):
-        kv_copy(j, j).wait_recv()
-        q_copy(j, j).wait_recv()
-
-    peers(wait_qkv, S, me)
+    def hand(i, c):
+        src = lax.rem(mine + i, HEADS) * group + member
+        kv_wait(src, src)
+        for e in range(1, group):
+            kv_hand(src, i, e).start()
+        return c
+
+    lax.fori_loop(1, HEADS, hand, 0)
+    peers(lambda j: q_copy(j, j).wait_recv(), S, me)
+
+    def handed(i, c):
+        for e in range(1, group):
+            giver = lax.rem(member + e, group)
+            kv_wait(i * group + giver, lead + giver)
+        return c
+
+    lax.fori_loop(0, HEADS, handed, 0)
     gather_step(1)
 
     owners = max(1, 256 // part)
@@ -194,6 +242,8 @@
     lax.fori_loop(blocks // 2, blocks, attend, 0)
     for n in range(3, len(bits)):
         gather_step(n)
+    for load in loads[4:]:
+        load.wait()
     atr[me] = ats[me]
     dkf[0:KW] = dk_ref[...].astype(F32)
 
@@ -343,6 +393,7 @@
         mid_ref[...].astype(F32)
         + jnp.dot(act_ref[...], co_ref[...], preferred_element_type=F32)
     ).astype(BF16)
+    stores[0].start()
 
     halo(2, "wait")
     place(2, cp)
@@ -397,6 +448,7 @@
     )
     gm = (ct_ref[...].astype(F32) + rscale * inner).astype(BF16)
     gm_ref[...] = gm
+    stores[1].start()
 
     att_t = att_ref[...].T
     nc = model // DPN
@@ -433,6 +485,8 @@
         n = min(8, KW - r0)
         gk_ref[r0:r0 + n, c0:c0 + kc] = gk3r[j][:n]
 
+    stores[3].start()
+
     peers(lambda j: go(j, j).wait_recv(), S, me)
     acc = gor[0].astype(F32)
     for j in range(1, S):
@@ -445,7 +499,6 @@
     peers(lambda j: gf(j, dp).start(), DPN, dp)
 
     def close(j):
-        kv_copy(j, me).wait_send()
         q_copy(j, me).wait_send()
         at_copy(j, me).wait_send()
         k1(j, me).wait_send()
@@ -453,7 +506,16 @@
         go(j, me).wait_send()
 
     peers(close, S, me)
-    for o, order in enumerate((order_a, order_b)):
+    peers(lambda h: kv_copy(h).wait_send(), HEADS, mine)
+
+    def close_hand(i, c):
+        src = lax.rem(mine + i, HEADS) * group + member
+        for e in range(1, group):
+            kv_hand(src, i, e).wait_send()
+        return c
+
+    lax.fori_loop(0, HEADS, close_hand, 0)
+    for o, order in enumerate(orders):
         for n in range(len(bits)):
             for r in subsets(order, n):
                 w_copy(o, r, order[n]).wait_send()
@@ -466,6 +528,7 @@
     peers(lambda j: gf(j, j).wait_recv(), DPN, dp)
     for d in range(DPN):
         go_ref[:, d * nc:(d + 1) * nc] = gofr[d]
+    stores[2].start()
 
     def close_dp(j):
         k2(j, dp).wait_send()
@@ -473,6 +536,27 @@
         gf(j, dp).wait_send()
 
     peers(close_dp, DPN, dp)
+    for store in stores:
+        store.wait()
+
+
+def hand_on(a, b, c, d, a_out, b_out, c_out, d_out, ab, bb, cb, db, in_sem, out_sem):
+    held = [ab, bb, cb, db]
+    loads = [
+        pltpu.make_async_copy(src, buf, in_sem.at[n])
+        for n, (src, buf) in enumerate(zip([a, b, c, d], held))
+    ]
+    stores = [
+        pltpu.make_async_copy(buf, dst, out_sem.at[n])
+        for n, (buf, dst) in enumerate(zip(held, [a_out, b_out, c_out, d_out]))
+    ]
+    for load in loads:
+        load.start()
+    for load, store in zip(loads, stores):
+        load.wait()
+        store.start()
+    for store in stores:
+        store.wait()
 
 
 def body(queries, keys, values, residual, out_proj, conv_in, conv_out, depth_kernel, norm_gain,
@@ -492,6 +576,11 @@
     wide = V((rows, model), F32)
     slim = V((rows, model), BF16)
     scratch = [
+        V((rows, width), BF16), V((rows, width), BF16), V((rows, width), BF16), slim,
+        V((width, model), BF16), V((model, model), BF16), V((KW, model), BF16),
+        V((1, model), F32), slim,
+        slim, slim, V((orow, model), F32), V((KW, model), F32),
+        D((10,)), D((4,)), D((HEADS, group)),
         V((HEADS, rows, 2 * DH), BF16), V((S, rows, 2 * DH), BF16),
         V((S, part, 2 * DH), BF16), V((S, part, 2 * DH), BF16),
         V((S, part, 2 * DH), BF16), V((S, part, 2 * DH), BF16),
@@ -503,21 +592,22 @@
         V((8, kc), F32), V((DPN, 8, kc), F32), V((S, 8, kc), F32),
         V((DPN, S, orow, nc), BF16), V((DPN, S, orow, nc), BF16),
         V((S, orow, nc), BF16), V((S, orow, nc), BF16), V((DPN, orow, nc), F32),
-        D((S,)), D((S,)), D((S,)), D((S,)), D((S,)), D((S,)), D((2, S)), D((2, S)), D((S,)), D((S,)),
+        D((HEADS,)), D((S,)), D((S,)), D((S,)), D((S,)), D((S,)), D((8, S)), D((8, S)), D((S,)), D((S,)),
         D((4,)), D((4,)), D((S,)), D((S,)), D((DPN,)), D((DPN,)), D((S,)), D((S,)),
         D((DPN,)), D((DPN,)), D((S,)), D((S,)), D((DPN,)), D((DPN,)),
     ]
-    vm = pl.BlockSpec(memory_space=pltpu.VMEM)
-    lo, gm, go, gk = pl.pallas_call(
+    anywhere = pl.BlockSpec(memory_space=pl.ANY)
+    shapes = [
+        jax.ShapeDtypeStruct((rows, model), BF16),
+        jax.ShapeDtypeStruct((rows, model), BF16),
+        jax.ShapeDtypeStruct((orow, model), F32),
+        jax.ShapeDtypeStruct((KW, model), F32),
+    ]
+    results = pl.pallas_call(
         functools.partial(kernel, S, DPN),
-        out_shape=[
-            jax.ShapeDtypeStruct((rows, model), BF16),
-            jax.ShapeDtypeStruct((rows, model), BF16),
-            jax.ShapeDtypeStruct((orow, model), F32),
-            jax.ShapeDtypeStruct((KW, model), F32),
-        ],
-        in_specs=[vm] * 10,
-        out_specs=[vm] * 4,
+        out_shape=shapes,
+        in_specs=[anywhere] * 10,
+        out_specs=[anywhere] * 4,
         scratch_shapes=scratch,
         compiler_params=pltpu.CompilerParams(
             collective_id=0, has_side_effects=True, vmem_limit_bytes=60 * 1024 * 1024
@@ -526,6 +616,13 @@
         queries[0], keys[0], values[0], residual[0], out_proj, conv_in, conv_out, depth_kernel,
         norm_gain.reshape(1, model), cotangent[0],
     )
+    lo, gm, go, gk = pl.pallas_call(
+        hand_on,
+        out_shape=shapes,
+        in_specs=[anywhere] * 4,
+        out_specs=[anywhere] * 4,
+        scratch_shapes=[V(x.shape, x.dtype) for x in shapes] + [D((4,)), D((4,))],
+    )(*results)
     return lo[None], gm[None], go, gk
 
 

time: 109 us -> 90.2 us (0.83)
  Pallas kernels: 102 us -> 89.4 us
  local copies, waits for them, and re-layouts: 6.47 us -> 0 us
    pallas_call x1 -> x2, Pallas kernels: 102 us -> 89.4 us  [the longest x1 87.5 us: body(): pl.pallas_call(functools.partial(kernel, S, DPN), out_shape=shapes, in_sp...]
    unnamed x4 -> x0, local copies, waits for them, and re-layouts: 6.47 us -> none
where the time goes in v2:
time: 90.2 us; the launch traced here: 90.1 us
  Pallas kernels  89.4 us (99%)
    pallas_call x1, Pallas kernels, body(): pl.pallas_call(functools.partial(kernel, S, DPN), out_shape=shapes, in_sp...  87.5 us
    pallas_call x1, Pallas kernels, body(): pl.pallas_call(hand_on, out_shape=shapes, in_specs=[anywhere] * 4, out_sp...  1.89 us

profile of v2, /device:TPU:13, one launch (start us, length us, event | category | flops | bytes accessed | tf_op | source)
XLA Modules:
  0.0 90.1 jit_solution(18208673450527410525)
XLA Ops:
  0.6 87.5 %shard_map.129 = (bf16[128,1024]{1,0:T(8,128)(2,1)}, bf16[128,1024]{1,0:T(8,128)(2,1)}, f32[32,1024]{1,0:T(8,128)}, f32[31,1024]{1,0:T(8,128)}) custom-call(bf16[128,512]{1,0:T(8,128)(2,1)} %bitcast.10, bf16[128,512]{1,0:T(8,128)(2,1)} %bitcast.11, bf16[128,512]{1,0:T(8,128)(2,1)} %bitcast.12, bf16[128,1024]{1,0:T(8,128)(2,1)} %bitcast.8, ...), custom_call_target="tpu_custom_call" | custom-call | tf_op jit(solution)/shard_map/pallas_call | solution.py:606
  88.2 1.9 %shard_map.130 = (bf16[128,1024]{1,0:T(8,128)(2,1)}, bf16[128,1024]{1,0:T(8,128)(2,1)}, f32[32,1024]{1,0:T(8,128)}, f32[31,1024]{1,0:T(8,128)}) custom-call(bf16[128,1024]{1,0:T(8,128)(2,1)} %get-tuple-element.12.a, bf16[128,1024]{1,0:T(8,128)(2,1)} %get-tuple-element.13.b, f32[32,1024]{1,0:T(8,128)} %get-tuple-element.14.c, f32[31,1024]{1,0:T(8,128)} %get-tuple-element.15.d), custom_call_target="tpu_custom_call" | custom-call | tf_op jit(solution)/shard_map/pallas_call | solution.py:619

commit v3 on v2

--- a/solution.py
+++ b/solution.py
@@ -50,6 +50,7 @@
     rows, model = res_in.shape
     group = S // HEADS
     part = rows // group
+    packed = part % 32 == 0
     cw = ci_in.shape[1]
     member = lax.rem(me, group)
     lead = me - member
@@ -113,7 +114,10 @@
         kvs[h] = jnp.concatenate([k_ref[:, cols], v_ref[:, cols]], axis=1)
         for g in range(group):
             piece = q_ref[g * part:(g + 1) * part, cols] * jnp.asarray(DH ** -0.5, BF16)
-            qs[h * group + g] = jnp.concatenate([piece, zeros64], axis=1)
+            if packed:
+                qs[h * group + g] = jnp.concatenate([piece[:part // 2], piece[part // 2:]], axis=1)
+            else:
+                qs[h * group + g] = jnp.concatenate([piece, zeros64], axis=1)
     pl.semaphore_wait(barrier, S - 1 + DPN - 1)
 
     def kv_copy(h):
@@ -200,6 +204,8 @@
     lax.fori_loop(1, HEADS, hand, 0)
     peers(lambda j: q_copy(j, j).wait_recv(), S, me)
 
+    gather_step(1)
+
     def handed(i, c):
         for e in range(1, group):
             giver = lax.rem(member + e, group)
@@ -207,8 +213,6 @@
         return c
 
     lax.fori_loop(0, HEADS, handed, 0)
-    gather_step(1)
-
     owners = max(1, 256 // part)
     blocks = S // owners
     kv = kvr[...].reshape(S * rows, 2 * DH)
@@ -218,13 +222,25 @@
 
     def attend(i, c):
         first = i * owners
-        q = qr[pl.ds(first, owners)].reshape(owners * part, 2 * DH)
+        q = qr[pl.ds(first, owners)]
+        if packed:
+            blank = jnp.zeros((owners, part // 2, DH), BF16)
+            q = jnp.concatenate(
+                [
+                    jnp.concatenate([q[:, :, :DH], blank], axis=2),
+                    jnp.concatenate([q[:, :, DH:], blank], axis=2),
+                ],
+                axis=1,
+            )
+        q = q.reshape(owners * part, 2 * DH)
         s = lax.dot_general(q, kv, (((1,), (1,)), ((), ())), preferred_element_type=F32)
         top = jnp.max(s, axis=1, keepdims=True)
         e = jnp.exp(s - top)
         total = jnp.sum(e, axis=1, keepdims=True)
         mixed = jnp.dot(e.astype(BF16), kv, preferred_element_type=F32)
         out = (mixed / total).astype(BF16).reshape(owners, part, 2 * DH)
+        if packed:
+            out = jnp.concatenate([out[:, :part // 2, DH:], out[:, part // 2:, DH:]], axis=2)
         ats[pl.ds(first, owners)] = out
 
         def send(n, c2):
@@ -237,9 +253,9 @@
         lax.fori_loop(0, owners, send, 0)
         return c
 
-    lax.fori_loop(0, blocks // 2, attend, 0)
+    lax.fori_loop(0, blocks // 4, attend, 0)
     gather_step(2)
-    lax.fori_loop(blocks // 2, blocks, attend, 0)
+    lax.fori_loop(blocks // 4, blocks, attend, 0)
     for n in range(3, len(bits)):
         gather_step(n)
     for load in loads[4:]:
@@ -258,8 +274,13 @@
     peers(wait_at, S, me)
     for g in range(group):
         for h in range(0, HEADS, 2):
-            left = atr[h * group + g][:, DH:]
-            right = atr[(h + 1) * group + g][:, DH:]
+            left = atr[h * group + g]
+            right = atr[(h + 1) * group + g]
+            if packed:
+                left = jnp.concatenate([left[:, :DH], left[:, DH:]], axis=0)
+                right = jnp.concatenate([right[:, :DH], right[:, DH:]], axis=0)
+            else:
+                left, right = left[:, DH:], right[:, DH:]
             att_ref[g * part:(g + 1) * part, h * DH:(h + 2) * DH] = jnp.concatenate(
                 [left, right], axis=1
             )
@@ -567,6 +588,7 @@
     model = residual.shape[2]
     group = S // HEADS
     part = rows // group
+    lane_rows = part // 2 if part % 32 == 0 else part
     cw = conv_in.shape[1]
     kc = 32 * model // (8 * S)
     orow = width // S
@@ -582,8 +604,8 @@
         slim, slim, V((orow, model), F32), V((KW, model), F32),
         D((10,)), D((4,)), D((HEADS, group)),
         V((HEADS, rows, 2 * DH), BF16), V((S, rows, 2 * DH), BF16),
-        V((S, part, 2 * DH), BF16), V((S, part, 2 * DH), BF16),
-        V((S, part, 2 * DH), BF16), V((S, part, 2 * DH), BF16),
+        V((S, lane_rows, 2 * DH), BF16), V((S, lane_rows, 2 * DH), BF16),
+        V((S, lane_rows, 2 * DH), BF16), V((S, lane_rows, 2 * DH), BF16),
         V((S, model, cw), BF16),
         V((rows, width), BF16), slim, wide, wide, wide, slim, slim,
         V((rows + 32, model), F32), V((rows + 32, model), F32), V((rows, 2 * model), BF16),

time: 90.2 us -> 86.5 us (0.959)
  Pallas kernels: 89.4 us -> 85.5 us
    pallas_call x1, Pallas kernels: 87.5 us -> 83.6 us  [body(): pl.pallas_call(functools.partial(kernel, S, DPN), out_shape=shapes, in_sp...]
where the time goes in v3:
time: 86.5 us; the launch traced here: 86.2 us
  Pallas kernels  85.5 us (99%)
    pallas_call x1, Pallas kernels, body(): pl.pallas_call(functools.partial(kernel, S, DPN), out_shape=shapes, in_sp...  83.6 us
    pallas_call x1, Pallas kernels, body(): pl.pallas_call(hand_on, out_shape=shapes, in_specs=[anywhere] * 4, out_sp...  1.89 us

profile of v3, /device:TPU:13, one launch (start us, length us, event | category | flops | bytes accessed | tf_op | source)
XLA Modules:
  0.0 86.2 jit_solution(5698324624013663703)
XLA Ops:
  0.6 83.6 %shard_map.129 = (bf16[128,1024]{1,0:T(8,128)(2,1)}, bf16[128,1024]{1,0:T(8,128)(2,1)}, f32[32,1024]{1,0:T(8,128)}, f32[31,1024]{1,0:T(8,128)}) custom-call(bf16[128,512]{1,0:T(8,128)(2,1)} %bitcast.10, bf16[128,512]{1,0:T(8,128)(2,1)} %bitcast.11, bf16[128,512]{1,0:T(8,128)(2,1)} %bitcast.12, bf16[128,1024]{1,0:T(8,128)(2,1)} %bitcast.8, ...), custom_call_target="tpu_custom_call" | custom-call | tf_op jit(solution)/shard_map/pallas_call | solution.py:628
  84.3 1.9 %shard_map.130 = (bf16[128,1024]{1,0:T(8,128)(2,1)}, bf16[128,1024]{1,0:T(8,128)(2,1)}, f32[32,1024]{1,0:T(8,128)}, f32[31,1024]{1,0:T(8,128)}) custom-call(bf16[128,1024]{1,0:T(8,128)(2,1)} %get-tuple-element.12.a, bf16[128,1024]{1,0:T(8,128)(2,1)} %get-tuple-element.13.b, f32[32,1024]{1,0:T(8,128)} %get-tuple-element.14.c, f32[31,1024]{1,0:T(8,128)} %get-tuple-element.15.d), custom_call_target="tpu_custom_call" | custom-call | tf_op jit(solution)/shard_map/pallas_call | solution.py:641
